TPU v7x, 32 devices: a whole 2x2x4 slice. The times are simulated.
32 devices in a mesh: feat: 8 (over z, y), dp: 4 (over x, core).
Axes of the slice: x: 2, y: 2, z: 4, core: 2. Of those that a mesh axis runs over, the one named last changes fastest.
Arguments:
- face_grid: bfloat16 [4096, 10240], P('dp', 'feat'), may hold values from -6 to 6
- first_nbrs: int32 [2048, 8], P('dp'), may hold values from 0 to 1023
- first_count: int32 [2048], P('dp'), may hold values from 1 to 8
- w_first: bfloat16 [10240, 256], P('feat'), may hold values from -0.0625 to 0.0625
- b_first: float32 [256], replicated, may hold values from -3 to 3
- send_rows: int32 [512], P('dp'), may hold values from 0 to 511
- second_nbrs: int32 [2048, 8], P(('dp', 'feat')), may hold values from 0 to 639
- second_count: int32 [2048], P(('dp', 'feat')), may hold values from 1 to 8
- w_in: bfloat16 [256, 1024], replicated, may hold values from -0.375 to 0.375
- w_out: bfloat16 [1024, 256], replicated, may hold values from -0.1875 to 0.1875
- out_grad: bfloat16 [2048, 256], P(('dp', 'feat')), may hold values from -6 to 6
Outputs:
- embed: bfloat16 [2048, 256], P(('dp', 'feat'))
- grad_first: float32 [10240, 256], P('feat')
Inputs may be any that keep to these rules, and one draw needn't show every extreme that they name: `first_count`: slots at or past a target's count are ignored; counts lie in 1 to 8. `first_nbrs`: only slots below first_count are read. `second_count`: slots at or past a target's count are ignored. `second_nbrs`: indices below 512 name the partition's own targets, the rest the faces received from the previous partition in order; only slots below second_count are read. `send_rows`: entries may repeat.
All inputs are finite; a program needn't handle non-finite values.
Results may differ from a plain program's by a relative error of at most 0.0061.
Values may be sent and summed in bfloat16 or wider, within the bound.
A program may use at most 64 MiB of HBM per device.

v0:
```python
import jax
import jax.numpy as jnp
from jax import lax
from jax.sharding import PartitionSpec as P


def passed_along(shard, axis, by):
    devices = lax.axis_size(axis)
    return lax.ppermute(shard, axis, [(i, (i + by) % devices) for i in range(devices)])


def slope(value):
    sig = jax.nn.sigmoid(value)
    return sig * (1.0 + value * (1.0 - sig))


def mean_rows(table, nbrs, count):
    total = jnp.zeros((nbrs.shape[0], table.shape[1]), jnp.float32)
    for slot in range(nbrs.shape[1]):
        picked = table[nbrs[:, slot]].astype(jnp.float32)
        total = total + jnp.where((slot < count)[:, None], picked, 0.0)
    return total / count[:, None].astype(jnp.float32)


def spread(grad, nbrs, count, size):
    slots = jnp.arange(nbrs.shape[1], dtype=jnp.int32)
    factor = jnp.where(
        slots[None, :] < count[:, None], 1.0 / count[:, None].astype(jnp.float32), 0.0
    )
    terms = (grad[:, None, :] * factor[:, :, None]).reshape(-1, grad.shape[1])
    return jax.ops.segment_sum(terms, nbrs.reshape(-1), num_segments=size)


def body(
    face_grid,
    first_nbrs,
    first_count,
    w_first,
    b_first,
    send_rows,
    second_nbrs,
    second_count,
    w_in,
    w_out,
    out_grad,
):
    targets = first_nbrs.shape[0]
    agg_first = (
        face_grid[:targets].astype(jnp.float32) + mean_rows(face_grid, first_nbrs, first_count)
    ).astype(jnp.bfloat16)
    partial_value = jnp.dot(agg_first, w_first, preferred_element_type=jnp.float32)
    pre_own = lax.psum_scatter(partial_value, "feat", scatter_dimension=0, tiled=True) + b_first
    hidden_own = jax.nn.silu(pre_own).astype(jnp.bfloat16)
    table = lax.all_gather(hidden_own, "feat", axis=0, tiled=True)
    received = passed_along(table[send_rows], "dp", 1)
    extended = jnp.concatenate([table, received], axis=0)
    agg_second = (
        hidden_own.astype(jnp.float32) + mean_rows(extended, second_nbrs, second_count)
    ).astype(jnp.bfloat16)
    pre_mlp = jnp.dot(agg_second, w_in, preferred_element_type=jnp.float32)
    act_mlp = jax.nn.silu(pre_mlp).astype(jnp.bfloat16)
    embed = (
        hidden_own.astype(jnp.float32) + jnp.dot(act_mlp, w_out, preferred_element_type=jnp.float32)
    ).astype(jnp.bfloat16)
    grad_act = lax.dot_general(
        out_grad, w_out, (((1,), (1,)), ((), ())), preferred_element_type=jnp.float32
    )
    grad_pre_mlp = (grad_act * slope(pre_mlp)).astype(jnp.bfloat16)
    grad_agg = lax.dot_general(
        grad_pre_mlp, w_in, (((1,), (1,)), ((), ())), preferred_element_type=jnp.float32
    )
    grad_ext = spread(grad_agg, second_nbrs, second_count, extended.shape[0])
    full_rows = table.shape[0]
    returned = passed_along(grad_ext[full_rows:].astype(jnp.bfloat16), "dp", -1).astype(jnp.float32)
    table_grad = grad_ext[:full_rows].at[send_rows].add(returned)
    own_terms = out_grad.astype(jnp.float32) + grad_agg
    grad_own = (
        lax.psum_scatter(
            table_grad.astype(jnp.bfloat16), "feat", scatter_dimension=0, tiled=True
        ).astype(jnp.float32)
        + own_terms
    )
    grad_pre_own = (grad_own * slope(pre_own)).astype(jnp.bfloat16)
    grad_pre_first = lax.all_gather(grad_pre_own, "feat", axis=0, tiled=True)
    slice_grad = lax.dot_general(
        agg_first, grad_pre_first, (((0,), (0,)), ((), ())), preferred_element_type=jnp.float32
    )
    grad_first = lax.psum(slice_grad, "dp")
    return (embed, grad_first)


def solution(mesh):
    return jax.shard_map(
        body,
        mesh=mesh,
        in_specs=(
            P("dp", "feat"),
            P("dp", None),
            P("dp"),
            P("feat", None),
            P(),
            P("dp"),
            P(("dp", "feat"), None),
            P(("dp", "feat")),
            P(),
            P(),
            P(("dp", "feat"), None),
        ),
        out_specs=(P(("dp", "feat"), None), P("feat", None)),
        check_vma=False,
    )
```

profile of v0, /device:TPU:0, one launch (start us, length us, event | category | flops | bytes accessed | tf_op | source)
XLA Modules:
  0.0 301.2 jit_solution(9618422344778929595)
XLA Ops:
  7.2 0.0 copy-start
  7.2 0.0 reduce-scatter.3.cloned.1.call-start
  7.2 0.7 broadcast_compare_fusion.7
  8.0 0.7 convert_element_type.107
  8.7 1.0 compare_select_fusion.7
  9.7 0.0 copy-start.1
  9.7 6.2 %gather_fusion = bf16[512,1280]{1,0:T(8,128)(2,1)} fusion(bf16[1024,1280]{1,0:T(8,128)(2,1)} %param.11, s32[1024]{0:T(1024)S(1)} %get-tuple-element.49), kind=kCustom, calls=%fused_computation | custom fusion | bytes 2623488 | tf_op jit(solution)/shard_map/gather | solution.py:20
  15.9 2.9 gather_fusion.1
  18.8 2.9 gather_fusion.2
  21.7 2.9 gather_fusion.3
  24.6 2.9 gather_fusion.4
  27.5 2.9 gather_fusion.5
  30.3 2.9 gather_fusion.6
  33.2 2.9 gather_fusion.7
  36.1 5.7 %add_convert_fusion = bf16[512,1280]{1,0:T(8,128)(2,1)S(1)} fusion(bf16[512,1280]{1,0:T(8,128)(2,1)} %gather_fusion.7, bf16[512,1280]{1,0:T(8,128)(2,1)} %gather_fusion.6, bf16[512,1280]{1,0:T(8,128)(2,1)} %gather_fusion.5, bf16[512,1280]{1,0:T(8,128)(2,1)} %gather_fusion.4, bf16[512,1280]{1,0:T(8,128)(2,1)} %gather_fusion.3, ...), kind=kLoop, calls=%fused_computation.19 | loop fusion | flops 17694720 | bytes 13113344 | tf_op jit(solution)/shard_map/convert_element_type | solution.py:50
  41.8 0.0 copy-start.2
  41.8 1.0 copy-done.2
  42.9 0.0 copy-start.7
  42.9 1.3 fusion.40
  44.2 0.0 reduce-scatter.3.cloned.1.call-update
  44.2 0.0 reduce-scatter.5.cloned.1.call-start
  44.3 0.0 copy-done.8
  44.3 0.1 fusion.28
  44.4 0.1 select_n.163
  44.5 0.0 copy-done.6
  44.5 0.1 copy.13
  44.6 0.1 reshape.203
  44.8 64.2 %reduce-scatter.3.cloned.1.call-done = f32[64,256]{1,0:T(8,128)} async-done(((f32[512,256]{1,0:T(8,128)}), f32[64,256]{1,0:T(8,128)}) %reduce-scatter.3.cloned.1.call-update) | async-done | bytes 65552 | tf_op jit(solution)/shard_map/reduce_scatter | solution.py:52
  109.0 0.0 copy-done.7
  109.0 0.9 multiply_convert_fusion.3
  109.8 31.0 %all_gather.6 = bf16[512,256]{1,0:T(8,128)(2,1)S(1)} all-gather(bf16[64,256]{1,0:T(8,128)(2,1)S(1)} %multiply_convert_fusion.3), channel_id=1, replica_groups=mesh['feat'=8,'dp'=4] {'feat'}, dimensions={0}, use_global_device_ids=true | all-gather | bytes 294912 | tf_op jit(solution)/shard_map/all_gather | solution.py:54
  140.8 0.8 gather_fusion.8
  141.6 0.2 collective-permute-start
  141.9 0.0 copy-start.9
  141.9 3.6 %collective-permute-done = bf16[128,256]{1,0:T(8,128)(2,1)S(1)} collective-permute-done((bf16[128,256]{1,0:T(8,128)(2,1)S(1)}, bf16[128,256]{1,0:T(8,128)(2,1)S(1)}, u32[]{:S(2)}, u32[]{:S(2)}) %collective-permute-start) | collective-permute-done | bytes 65568 | tf_op jit(solution)/shard_map/ppermute | solution.py:9
  145.6 0.7 gather_fusion.10
  146.3 0.7 gather_fusion.11
  147.0 0.7 gather_fusion.12
  147.7 0.0 copy-start.5
  147.7 0.0 copy-start.10
  147.7 0.7 gather_fusion.13
  148.4 0.7 gather_fusion.14
  149.1 0.7 gather_fusion.15
  149.8 0.7 gather_fusion.9
  150.5 0.7 gather_fusion.16
  151.2 0.3 fusion.16
  151.5 0.5 fusion.1
  152.1 3.6 %scatter_custom_fusion = f32[640,256]{1,0:T(8,128)S(1)} fusion(s32[512]{0:T(512)S(1)} %reshape.203, f32[]{:T(128)} %constant.15.clone.1, f32[512]{0:T(512)S(1)} %select_n.163, f32[64,256]{1,0:T(8,128)S(1)} %fusion.1), kind=kCustom, calls=%fused_computation.26 | custom fusion | flops 262144 | bytes 722948 | tf_op jit(solution)/shard_map/scatter-add | solution.py:31
  155.7 0.0 copy-start.4
  155.7 0.1 collective-permute-start.1
  155.8 0.0 copy-start.3
  155.8 1.8 collective-permute-done.1
  157.7 1.5 scatter_custom_fusion.1
  159.2 0.7 convert_element_type.125
  159.9 0.0 reduce-scatter.5.cloned.1.call-update
  159.9 0.0 all-reduce.2.cloned.1.call-start
  160.0 60.7 %reduce-scatter.5.cloned.1.call-done = bf16[64,256]{1,0:T(8,128)(2,1)} async-done(((bf16[512,256]{1,0:T(8,128)(2,1)}), bf16[64,256]{1,0:T(8,128)(2,1)}) %reduce-scatter.5.cloned.1.call-update) | async-done | bytes 32784 | tf_op jit(solution)/shard_map/reduce_scatter | solution.py:78
  220.7 0.8 multiply_convert_fusion.2
  221.5 30.9 %all_gather.7 = bf16[512,256]{1,0:T(8,128)(2,1)S(1)} all-gather(bf16[64,256]{1,0:T(8,128)(2,1)S(1)} %multiply_convert_fusion.2), channel_id=1, replica_groups=mesh['feat'=8,'dp'=4] {'feat'}, dimensions={0}, use_global_device_ids=true | all-gather | bytes 294912 | tf_op jit(solution)/shard_map/all_gather | solution.py:84
  252.4 1.6 fusion.41
  254.0 0.0 all-reduce.2.cloned.1.call-update
  254.0 0.8 fusion.2
  254.8 37.3 %all-reduce.2.cloned.1.call-done = f32[1280,256]{1,0:T(8,128)} async-done(((f32[1280,256]{1,0:T(8,128)}), f32[1280,256]{1,0:T(8,128)}) %all-reduce.2.cloned.1.call-update) | async-done | bytes 1310736 | tf_op jit(solution)/shard_map/psum | solution.py:88
  292.2 2.5 copy.17
  (29 shorter events, 0.2 us)
Async XLA Ops:
  7.2 35.7 %copy-start = (bf16[1280,256]{1,0:T(8,128)(2,1)S(1)}, bf16[1280,256]{1,0:T(8,128)(2,1)}, u32[]{:S(2)}) copy-start(bf16[1280,256]{1,0:T(8,128)(2,1)} %param.14) | copy-start | bytes 1966084
  7.2 101.8 %reduce-scatter.3.cloned.1.call-start = ((), (), s32[]{:S(2)}) async-start(), calls=%async_computation.2 | async-start | bytes 589824 | tf_op jit(solution)/shard_map/reduce_scatter | solution.py:52
  9.7 6.2 %copy-start.1 = (bf16[1024,1280]{1,0:T(8,128)(2,1)S(1)}, bf16[1024,1280]{1,0:T(8,128)(2,1)}, u32[]{:S(2)}) copy-start(bf16[1024,1280]{1,0:T(8,128)(2,1)} %param.11) | copy-start | bytes 7864324
  41.8 1.1 copy-start.2
  42.9 1.4 copy-start.8
  42.9 1.5 copy-start.11
  42.9 1.6 copy-start.6
  42.9 66.1 %copy-start.7 = (f32[256]{0:T(256)S(1)}, f32[256]{0:T(256)}, u32[]{:S(2)}) copy-start(f32[256]{0:T(256)} %param.15) | copy-start | bytes 3076
  44.2 176.5 %reduce-scatter.5.cloned.1.call-start = ((), (), s32[]{:S(2)}) async-start(), calls=%async_computation.3 | async-start | bytes 294912 | tf_op jit(solution)/shard_map/reduce_scatter | solution.py:78
  141.6 3.9 %collective-permute-start = (bf16[128,256]{1,0:T(8,128)(2,1)S(1)}, bf16[128,256]{1,0:T(8,128)(2,1)S(1)}, u32[]{:S(2)}, u32[]{:S(2)}) collective-permute-start(bf16[128,256]{1,0:T(8,128)(2,1)S(1)} %gather_fusion.8), channel_id=1, source_target_pairs={{0,1},{1,2},{2,3},{3,0},{4,5},{5,6},{6,7},{7,4},{8,9},{9,10},{10,1... | collective-permute-start | bytes 196616 | tf_op jit(solution)/shard_map/ppermute | solution.py:9
  141.9 9.3 %copy-start.9 = (bf16[256,1024]{1,0:T(8,128)(2,1)S(1)}, bf16[256,1024]{1,0:T(8,128)(2,1)}, u32[]{:S(2)}) copy-start(bf16[256,1024]{1,0:T(8,128)(2,1)} %param.19) | copy-start | bytes 1572868
  147.7 3.8 %copy-start.5 = (bf16[64,256]{1,0:T(8,128)(2,1)S(1)}, bf16[64,256]{1,0:T(8,128)(2,1)}, u32[]{:S(2)}) copy-start(bf16[64,256]{1,0:T(8,128)(2,1)} %param.21) | copy-start | bytes 98308
  147.7 3.8 %copy-start.10 = (bf16[1024,256]{1,0:T(8,128)(2,1)S(1)}, bf16[1024,256]{1,0:T(8,128)(2,1)}, u32[]{:S(2)}) copy-start(bf16[1024,256]{1,0:T(8,128)(2,1)} %param.20) | copy-start | bytes 1572868
  155.7 65.0 %copy-start.4 = (f32[64,256]{1,0:T(8,128)S(1)}, f32[64,256]{1,0:T(8,128)}, u32[]{:S(2)}) copy-start(f32[64,256]{1,0:T(8,128)} %reduce-scatter.3.cloned.1.call-done) | copy-start | bytes 196612
  155.7 2.0 collective-permute-start.1
  155.8 96.5 %copy-start.3 = (bf16[512,1280]{1,0:T(8,128)(2,1)S(1)}, bf16[512,1280]{1,0:T(8,128)(2,1)}, u32[]{:S(2)}) copy-start(bf16[512,1280]{1,0:T(8,128)(2,1)} %copy-done.2) | copy-start | bytes 3932164
  159.9 132.3 %all-reduce.2.cloned.1.call-start = ((), (), s32[]{:S(2)}) async-start(), calls=%async_computation.4 | async-start | bytes 2621440 | tf_op jit(solution)/shard_map/psum | solution.py:88
Sparse Core Ops, SparseCore 0:
  44.3 64.5 reduce-scatter.2
  160.0 60.5 reduce-scatter.4
  254.1 38.0 all-reduce.1
where the time goes:
time: 302 us; the launch traced here: 301 us
  waiting for transfers between devices  168 us (56%)
  blocking collectives  61.8 us (20%)
  local copies, waits for them, and re-layouts  36.7 us (12%)
  other arithmetic  15.8 us (5%)
  between operations  14.1 us (5%)
  matrix products  4.58 us (2%)
    reduce_scatter x1, waiting for transfers between devices, body(): lax.psum_scatter(partial_value, 'feat', scatter_dimension=0, tiled=True)  64.2 us
    reduce_scatter x1, waiting for transfers between devices, body(): lax.psum_scatter(table_grad.astype(jnp.bfloat16), 'feat', scatter_dimensi...  60.7 us
    psum x1, waiting for transfers between devices, body(): grad_first = lax.psum(slice_grad, 'dp')  37.3 us
    gather x16, local copies, waits for them, and re-layouts, mean_rows(): picked = table[nbrs[:, slot]].astype(jnp.float32)  31.9 us
    all_gather x1, blocking collectives, body(): table = lax.all_gather(hidden_own, 'feat', axis=0, tiled=True)  31 us
    all_gather x1, blocking collectives, body(): grad_pre_first = lax.all_gather(grad_pre_own, 'feat', axis=0, tiled=True)  30.9 us
  transfers between devices with their start and end apart: 5, of which 5 were waited for; matrix products, arithmetic and copies ran while one was open for 0% of the time, Pallas kernels for 0%

commit v1 on v0

v1 whole, which is shorter than its diff:
```python
import functools

import jax
import jax.numpy as jnp
from jax import lax
from jax.experimental import pallas as pl
from jax.experimental.pallas import tpu as pltpu
from jax.sharding import PartitionSpec as P

MESH = pl.DeviceIdType.MESH
F32, BF16 = jnp.float32, jnp.bfloat16


def dot(a, b):
    return jnp.dot(a, b, preferred_element_type=F32)


def dot_first(a, b):
    return lax.dot_general(a, b, (((0,), (0,)), ((), ())), preferred_element_type=F32)


def dot_last(a, b):
    return lax.dot_general(a, b, (((1,), (1,)), ((), ())), preferred_element_type=F32)


def slope(value):
    sig = jax.nn.sigmoid(value)
    return sig * (1.0 + value * (1.0 - sig))


def steps(count, fn):
    if count <= 2:
        for i in range(count):
            fn(i)
    else:
        pl.loop(0, count)(fn)


def split(size, width):
    return [(at, min(width, size - at)) for at in range(0, size, width)]


def counts_matrix(nbrs, source, out, at, rows, width):
    def group(g):
        names = nbrs[pl.ds(pl.multiple_of(source + g * 16, 16), 16), :8]
        for lane, size in split(width, 1024):
            spot = lax.broadcasted_iota(jnp.int32, (16, size), 1).astype(names.dtype) + lane
            total = jnp.zeros((16, size), F32)
            for slot in range(8):
                total = total + jnp.where(names[:, slot : slot + 1] == spot, 1.0, 0.0)
            out[pl.ds(pl.multiple_of(at + g * 16, 16), 16), lane : lane + size] = total.astype(BF16)

    pl.loop(0, rows // 16)(group)


def inverse(names):
    live = jnp.where(names >= 0, 1.0, 0.0)
    return 1.0 / jnp.sum(live, axis=1, keepdims=True)


def kernel(
    n, parts, block, chunks,
    face_hbm, nb1, w1_hbm, b1, srows, nb2, win_hbm, wout_hbm, og,
    embed, grad,
    face, w1, win, wout, adj, agg, agg_t, part32, part16, rs_buf, pre_own, pre_all,
    ext, picks, og_all, nb_pad, nb_send, nb_all, nb_nat, smat, grad_act, agg2, gscaled, gagg,
    halo_out, back_out, back_in, gtotal, gp, pair_out, pair_in, chip_buf,
    load_sem, rs_s, rs_r, ag_s, ag_r, og_s, og_r, nb_s, nb_r, halo_sem, back_sem,
    pa_s, pa_r, x_s, x_r, pb_s, pb_r,
):
    f, d = lax.axis_index("feat"), lax.axis_index("dp")
    src, width = face.shape
    targets, hid = nb1.shape[0], w1.shape[1]
    own = nb2.shape[0]
    halo = srows.shape[1]
    full = targets + halo
    mine = pl.ds(pl.multiple_of(f * own, own), own)
    cols = split(width, 256)

    loads = [
        pltpu.make_async_copy(face_hbm.at[:, pl.ds(at, size)], face.at[:, pl.ds(at, size)], load_sem.at[i])
        for i, (at, size) in enumerate(cols)
    ]
    loads.append(pltpu.make_async_copy(w1_hbm, w1, load_sem.at[len(cols)]))
    late = [
        pltpu.make_async_copy(wout_hbm, wout, load_sem.at[len(cols) + 1]),
        pltpu.make_async_copy(win_hbm, win, load_sem.at[len(cols) + 2]),
    ]
    for copy in loads + late:
        copy.start()

    barrier = pltpu.get_barrier_semaphore()
    for i in range(1, n):
        pl.semaphore_signal(barrier, inc=1, device_id={"feat": lax.rem(f + i, n)}, device_id_type=MESH)
    for i in range(1, parts):
        pl.semaphore_signal(barrier, inc=1, device_id={"dp": lax.rem(d + i, parts)}, device_id_type=MESH)

    nb_pad[...] = jnp.full(nb_pad.shape, -1.0, F32)
    nb_pad[:own, :8] = nb2[...].astype(F32)
    nb_send[...] = jnp.transpose(nb_pad[...])[:8]
    if nb_all.shape[0] > n * 8:
        nb_all[n * 8 :, :] = jnp.full((nb_all.shape[0] - n * 8, 128), -1.0, F32)
    nb_all[pl.ds(pl.multiple_of(f * 8, 8), 8), :] = nb_send[...]
    og_all[mine, :] = og[...]
    picks[...] = jnp.where(
        lax.broadcasted_iota(jnp.int32, (targets, halo), 0) == srows[...], 1.0, 0.0
    ).astype(BF16)

    pl.semaphore_wait(barrier, n - 1 + parts - 1)

    def gathered(source, buffer, rows, sends, recvs):
        place = buffer.at[pl.ds(pl.multiple_of(f * rows, rows), rows)]
        copies = []
        for i in range(1, n):
            copies.append(
                pltpu.make_async_remote_copy(
                    source, place, sends.at[i], recvs.at[i],
                    device_id={"feat": lax.rem(f + i, n)}, device_id_type=MESH,
                )
            )
        for copy in copies:
            copy.start()
        return copies

    nb_copies = gathered(nb_send, nb_all, 8, nb_s, nb_r)
    og_copies = gathered(og, og_all, own, og_s, og_r)

    blocks = targets // block
    per = block // own
    first = lax.rem(f // per + 1, blocks)

    def send_to(dest):
        return pltpu.make_async_remote_copy(
            part16.at[pl.ds(pl.multiple_of(dest * own, own), own)], rs_buf.at[f],
            rs_s.at[dest], rs_r.at[f], device_id={"feat": dest}, device_id_type=MESH,
        )

    if blocks > 2:
        for copy in loads:
            copy.wait()

    def first_layer(i):
        at = pl.multiple_of(lax.rem(first + i, blocks) * block, block)
        rows = pl.ds(at, block)
        counts_matrix(nb1, at, adj, 0, block, src)
        inv = inverse(nb1[rows, :])
        total = jnp.zeros((block, hid), F32)
        for j, (lane, size) in enumerate(cols):
            if blocks <= 2 and i == 0:
                loads[j].wait()
                if j == 0:
                    loads[-1].wait()
            chunk = slice(lane, lane + size)
            value = dot(adj[...], face[:, chunk]) * inv + face[rows, chunk].astype(F32)
            value = value.astype(BF16)
            agg[rows, chunk] = value
            total = total + dot(value, w1[chunk, :])
        part32[rows, :] = total
        part16[rows, :] = total.astype(BF16)
        for j in range(per):
            dest = lax.rem(first + i, blocks) * per + j
            pl.when(dest != f)(lambda dest=dest: send_to(dest).start())

    steps(blocks, first_layer)

    for lane, size in cols:
        agg_t[lane : lane + size, :] = jnp.transpose(agg[:, lane : lane + size])
    for copy in nb_copies:
        copy.wait()
    for at in range(0, nb_all.shape[0], 128):
        turned = jnp.transpose(nb_all[at : at + 128, :])
        for j in range(min(16, n - at // 8)):
            t = at // 8 + j
            nb_nat[t * own : (t + 1) * own, :8] = turned[:own, j * 8 : j * 8 + 8]
    counts_matrix(nb_nat, 0, smat, 0, targets, full)
    for copy in late + og_copies:
        copy.wait()

    def out_part(i):
        rows = pl.ds(pl.multiple_of(i * block, block), block)
        grad_act[rows, :] = dot_last(og_all[rows, :], wout[...])

    steps(blocks, out_part)

    value = part32[mine, :] + b1[...]
    for i in range(1, n):
        source = lax.rem(f + i, n)
        pltpu.make_async_remote_copy(
            part16.at[pl.ds(0, own)], rs_buf.at[source], rs_s.at[source], rs_r.at[source],
            device_id={"feat": source}, device_id_type=MESH,
        ).wait_recv()
        value = value + rs_buf[source].astype(F32)
    pre_own[...] = value.astype(BF16)
    pre_all[mine, :] = value.astype(BF16)
    for copy in gathered(pre_own, pre_all, own, ag_s, ag_r):
        copy.wait()

    ext[:targets, :] = jax.nn.silu(pre_all[...].astype(F32)).astype(BF16)
    halo_out[...] = dot_first(picks[...], ext[:targets, :]).astype(BF16)
    halo_copy = pltpu.make_async_remote_copy(
        halo_out, ext.at[pl.ds(targets, halo)], halo_sem.at[0], halo_sem.at[1],
        device_id={"dp": lax.rem(d + 1, parts)}, device_id_type=MESH,
    )
    halo_copy.start()

    def neighbour_part(i):
        rows = pl.ds(pl.multiple_of(i * block, block), block)
        gagg[rows, :] = dot(smat[rows, :targets], ext[:targets, :])

    steps(blocks, neighbour_part)
    halo_copy.wait()

    def second_layer(i):
        rows = pl.ds(pl.multiple_of(i * block, block), block)
        inv = inverse(nb_nat[rows, :8])
        total = gagg[rows, :] + dot(smat[rows, targets:], ext[targets:, :])
        value = (ext[rows, :].astype(F32) + total * inv).astype(BF16)
        agg2[rows, :] = value
        step = (grad_act[rows, :] * slope(dot(value, win[...]))).astype(BF16)
        back = dot_last(step, win[...])
        gagg[rows, :] = back
        gscaled[rows, :] = (back * inv).astype(BF16)

    steps(blocks, second_layer)

    back_out[...] = dot_first(smat[:, targets:], gscaled[...]).astype(BF16)
    back_copy = pltpu.make_async_remote_copy(
        back_out, back_in, back_sem.at[0], back_sem.at[1],
        device_id={"dp": lax.rem(d + parts - 1, parts)}, device_id_type=MESH,
    )
    back_copy.start()

    for at, size in split(targets, 512):
        rows = slice(at, at + size)
        gtotal[rows, :] = (
            og_all[rows, :].astype(F32) + gagg[rows, :] + dot_first(smat[:, rows], gscaled[...])
        )
    act = jax.nn.silu(dot(agg2[mine, :], win[...])).astype(BF16)
    embed[...] = (ext[mine, :].astype(F32) + dot(act, wout[...])).astype(BF16)

    back_copy.wait()
    gp[...] = (
        (gtotal[...] + dot(picks[...], back_in[...])) * slope(pre_all[...].astype(F32))
    ).astype(BF16)

    half = width // 2
    size = half // chunks
    side = lax.rem(d, 2)
    chip = d // 2
    chips = parts // 2
    mate = d + 1 - 2 * side

    def place(which, c):
        return pl.ds(pl.multiple_of(which * half + c * size, 16), size)

    pair_copies, chip_copies, end_copies = [], [], []
    for c in range(chunks):
        span = slice(c * size, (c + 1) * size)
        pair_out[span, :] = dot(agg_t[place(1 - side, c), :], gp[...]).astype(BF16)
        copy = pltpu.make_async_remote_copy(
            pair_out.at[pl.ds(c * size, size)], pair_in.at[pl.ds(c * size, size)], pa_s.at[c], pa_r.at[c],
            device_id={"dp": mate}, device_id_type=MESH,
        )
        copy.start()
        pair_copies.append(copy)
    for c in range(chunks):
        span = slice(c * size, (c + 1) * size)
        value = dot(agg_t[place(side, c), :], gp[...])
        pair_copies[c].wait()
        chip_buf[chip, span, :] = (value + pair_in[span, :].astype(F32)).astype(BF16)
        for i in range(1, chips):
            here = chip_buf.at[chip, pl.ds(c * size, size)]
            copy = pltpu.make_async_remote_copy(
                here, here, x_s.at[i, c], x_r.at[i, c],
                device_id={"dp": lax.rem(d + 2 * i, parts)}, device_id_type=MESH,
            )
            copy.start()
            chip_copies.append(copy)
    for c in range(chunks):
        span = slice(c * size, (c + 1) * size)
        for copy in chip_copies[c * (chips - 1) : (c + 1) * (chips - 1)]:
            copy.wait()
        total = chip_buf[0, span, :].astype(F32)
        for i in range(1, chips):
            total = total + chip_buf[i, span, :].astype(F32)
        grad[place(side, c), :] = total.astype(BF16)
        there = grad.at[place(side, c)]
        copy = pltpu.make_async_remote_copy(
            there, there, pb_s.at[c], pb_r.at[c], device_id={"dp": mate}, device_id_type=MESH,
        )
        copy.start()
        end_copies.append(copy)
    for copy in end_copies:
        copy.wait()
    for i in range(1, n):
        send_to(lax.rem(f + i, n)).wait_send()


def fused(n, parts, face_grid, nb1, w_first, b_first, send_rows, nb2, w_in, w_out, out_grad):
    src, width = face_grid.shape
    targets, hid = nb1.shape[0], w_first.shape[1]
    inner = w_in.shape[1]
    own, halo = nb2.shape[0], send_rows.shape[1]
    full = targets + halo
    block = min(targets, 256)
    half = width // 2
    chunks = next(c for c in (4, 2, 1) if (half // c) % 16 == 0)
    chips = parts // 2
    tiles = -(-n * 8 // 128) * 128
    any_space = pl.BlockSpec(memory_space=pl.ANY)
    vmem = pl.BlockSpec(memory_space=pltpu.VMEM)
    dma = pltpu.SemaphoreType.DMA
    return pl.pallas_call(
        functools.partial(kernel, n, parts, block, chunks),
        out_shape=(
            jax.ShapeDtypeStruct((own, hid), BF16),
            jax.ShapeDtypeStruct((width, hid), BF16),
        ),
        in_specs=[any_space, vmem, any_space, vmem, vmem, vmem, any_space, any_space, vmem],
        out_specs=(vmem, vmem),
        scratch_shapes=[
            pltpu.VMEM((src, width), BF16),
            pltpu.VMEM((width, hid), BF16),
            pltpu.VMEM((hid, inner), BF16),
            pltpu.VMEM((inner, hid), BF16),
            pltpu.VMEM((block, src), BF16),
            pltpu.VMEM((targets, width), BF16),
            pltpu.VMEM((width, targets), BF16),
            pltpu.VMEM((targets, hid), F32),
            pltpu.VMEM((targets, hid), BF16),
            pltpu.VMEM((n, own, hid), BF16),
            pltpu.VMEM((own, hid), BF16),
            pltpu.VMEM((targets, hid), BF16),
            pltpu.VMEM((full, hid), BF16),
            pltpu.VMEM((targets, halo), BF16),
            pltpu.VMEM((targets, hid), BF16),
            pltpu.VMEM((128, 128), F32),
            pltpu.VMEM((8, 128), F32),
            pltpu.VMEM((tiles, 128), F32),
            pltpu.VMEM((targets, 128), F32),
            pltpu.VMEM((targets, full), BF16),
            pltpu.VMEM((targets, inner), F32),
            pltpu.VMEM((targets, hid), BF16),
            pltpu.VMEM((targets, hid), BF16),
            pltpu.VMEM((targets, hid), F32),
            pltpu.VMEM((halo, hid), BF16),
            pltpu.VMEM((halo, hid), BF16),
            pltpu.VMEM((halo, hid), BF16),
            pltpu.VMEM((targets, hid), F32),
            pltpu.VMEM((targets, hid), BF16),
            pltpu.VMEM((half, hid), BF16),
            pltpu.VMEM((half, hid), BF16),
            pltpu.VMEM((chips, half, hid), BF16),
            dma((len(split(width, 256)) + 3,)),
            dma((n,)), dma((n,)), dma((n,)), dma((n,)), dma((n,)), dma((n,)), dma((n,)), dma((n,)),
            dma((2,)), dma((2,)),
            dma((chunks,)), dma((chunks,)),
            dma((chips, chunks)), dma((chips, chunks)),
            dma((chunks,)), dma((chunks,)),
        ],
        compiler_params=pltpu.CompilerParams(
            collective_id=0, has_side_effects=True, vmem_limit_bytes=56 * 1024 * 1024
        ),
        cost_estimate=pl.CostEstimate(
            flops=2 * targets * src * width, bytes_accessed=2 * src * width, transcendentals=0
        ),
        name="fused_step",
    )(face_grid, nb1, w_first, b_first, send_rows, nb2, w_in, w_out, out_grad)


def live(nbrs, count):
    slots = jnp.arange(nbrs.shape[1], dtype=jnp.int32)
    return jnp.where(slots[None, :] < count[:, None], nbrs, -1)


def solution(mesh):
    n, parts = mesh.shape["feat"], mesh.shape["dp"]

    def body(
        face_grid, first_nbrs, first_count, w_first, b_first, send_rows,
        second_nbrs, second_count, w_in, w_out, out_grad,
    ):
        embed, grad = fused(
            n, parts, face_grid, live(first_nbrs, first_count), w_first, b_first.reshape(1, -1),
            send_rows.reshape(1, -1), live(second_nbrs, second_count), w_in, w_out, out_grad,
        )
        return embed, grad.astype(F32)

    return jax.shard_map(
        body,
        mesh=mesh,
        in_specs=(
            P("dp", "feat"), P("dp", None), P("dp"), P("feat", None), P(), P("dp"),
            P(("dp", "feat"), None), P(("dp", "feat")), P(), P(), P(("dp", "feat"), None),
        ),
        out_specs=(P(("dp", "feat"), None), P("feat", None)),
        check_vma=False,
    )
```

time: 302 us -> 55.2 us (0.18)
  the two profiles are of different devices: /device:TPU:0 before, /device:TPU:25 now
where the time goes in v1:
time: 55.2 us; the launch traced here: 54.8 us
  Pallas kernels  46.1 us (84%)
  other arithmetic  5.11 us (9%)
  local copies, waits for them, and re-layouts  2.98 us (5%)
  between operations  0.65 us (1%)
    pallas_call x1, Pallas kernels, fused(): pl.pallas_call(functools.partial(kernel, n, parts, block, chunks), out_sh...  46.1 us
    unnamed x3, local copies, waits for them, and re-layouts  2.98 us
    select_n x2, other arithmetic, live(): return jnp.where(slots[None, :] < count[:, None], nbrs, -1)  2.87 us
    convert_element_type x1, other arithmetic, body(): return (embed, grad.astype(F32))  2.24 us

profile of v1, /device:TPU:25, one launch (start us, length us, event | category | flops | bytes accessed | tf_op | source)
XLA Modules:
  0.0 54.8 jit_solution(7188517775596089855)
XLA Ops:
  0.6 0.8 %copy.14 = s32[64,8]{1,0:T(8,128)S(1)} copy(s32[64,8]{0,1:T(8,128)} %param.17) | data formatting | bytes 4096 | tf_op args[6]
  1.4 1.3 %fusion.1.nb2 = s32[64,8]{1,0:T(8,128)} fusion(s32[64,8]{1,0:T(8,128)S(1)} %copy.14, s32[64]{0:T(128)} %param.18), kind=kLoop, calls=%fused_computation.3 | loop fusion | flops 1024 | bytes 4352 | tf_op jit(solution)/shard_map/jit(_where)/select_n | solution.py:373
  2.7 0.8 %copy.13 = s32[512,8]{1,0:T(8,128)S(1)} copy(s32[512,8]{0,1:T(8,128)} %param.12) | data formatting | bytes 32768 | tf_op args[1]
  3.6 1.5 %fusion.nb1 = s32[512,8]{1,0:T(8,128)} fusion(s32[512,8]{1,0:T(8,128)S(1)} %copy.13, s32[512]{0:T(512)} %param.13), kind=kLoop, calls=%fused_computation.1 | loop fusion | flops 8192 | bytes 34816 | tf_op jit(solution)/shard_map/jit(_where)/select_n | solution.py:373
  5.1 46.1 %fused_step.1 = (bf16[64,256]{1,0:T(8,128)(2,1)}, bf16[1280,256]{1,0:T(8,128)(2,1)}) custom-call(bf16[1024,1280]{1,0:T(8,128)(2,1)} %face_hbm.1, s32[512,8]{1,0:T(8,128)} %fusion.nb1, bf16[1280,256]{1,0:T(8,128)(2,1)} %w1_hbm.1, f32[1,256]{1,0:T(1,128)} %bitcast.2, s32[1,128]{1,0:T(1,128)} %bitcast.3, s32[64,8]{1,0:T(8,128)} %fusion.1.nb2, ...), custom_call_target="tpu_custom_call" | custom-call | flops 1342177280 | bytes 2621440 | tf_op jit(solution)/shard_map/fused_step/pallas_call | solution.py:313
  51.2 2.2 %convert_element_type.3 = f32[1280,256]{1,0:T(8,128)} convert(bf16[1280,256]{1,0:T(8,128)(2,1)} %get-tuple-element.5) | non-fusion elementwise | flops 327680 | bytes 1966080 | tf_op jit(solution)/shard_map/convert_element_type | solution.py:387
  53.5 1.4 %copy.16 = bf16[64,256]{1,0:T(8,128)(2,1)} copy(bf16[64,256]{1,0:T(8,128)(2,1)} %get-tuple-element.8) | data formatting | bytes 65536

commit v2 on v1

--- a/solution.py
+++ b/solution.py
@@ -15,16 +15,16 @@
     return jnp.dot(a, b, preferred_element_type=F32)
 
 
-def dot_first(a, b):
-    return lax.dot_general(a, b, (((0,), (0,)), ((), ())), preferred_element_type=F32)
-
-
 def dot_last(a, b):
     return lax.dot_general(a, b, (((1,), (1,)), ((), ())), preferred_element_type=F32)
 
 
+def sigmoid(value):
+    return 0.5 * jnp.tanh(0.5 * value) + 0.5
+
+
 def slope(value):
-    sig = jax.nn.sigmoid(value)
+    sig = sigmoid(value)
     return sig * (1.0 + value * (1.0 - sig))
 
 
@@ -41,16 +41,29 @@
 
 
 def counts_matrix(nbrs, source, out, at, rows, width):
+    spots = [
+        (lane, size, (lax.broadcasted_iota(jnp.int32, (8, size), 1) + lane).astype(F32))
+        for lane, size in split(width, 1024)
+    ]
+
     def group(g):
-        names = nbrs[pl.ds(pl.multiple_of(source + g * 16, 16), 16), :8]
-        for lane, size in split(width, 1024):
-            spot = lax.broadcasted_iota(jnp.int32, (16, size), 1).astype(names.dtype) + lane
-            total = jnp.zeros((16, size), F32)
-            for slot in range(8):
-                total = total + jnp.where(names[:, slot : slot + 1] == spot, 1.0, 0.0)
-            out[pl.ds(pl.multiple_of(at + g * 16, 16), 16), lane : lane + size] = total.astype(BF16)
+        for lane, size, spot in spots:
+            pieces = []
+            for piece in range(2):
+                names = nbrs[pl.ds(pl.multiple_of(source + g * 16 + piece * 8, 8), 8), :8]
+                total = jnp.zeros((8, size), F32)
+                for slot in range(8):
+                    total = total + jnp.where(names[:, slot : slot + 1] == spot, 1.0, 0.0)
+                pieces.append(total)
+            here = pl.ds(pl.multiple_of(at + g * 16, 16), 16)
+            out[here, lane : lane + size] = jnp.concatenate(pieces, axis=0).astype(BF16)
 
     pl.loop(0, rows // 16)(group)
+
+
+def live(nbrs, count):
+    slots = lax.broadcasted_iota(jnp.int32, nbrs.shape, 0)
+    return jnp.where(slots < count, nbrs, -1).astype(F32)
 
 
 def inverse(names):
@@ -60,10 +73,10 @@
 
 def kernel(
     n, parts, block, chunks,
-    face_hbm, nb1, w1_hbm, b1, srows, nb2, win_hbm, wout_hbm, og,
+    face_hbm, nb1_t, count1, w1_hbm, b1, srows, nb2_t, count2, win_hbm, wout_hbm, og,
     embed, grad,
     face, w1, win, wout, adj, agg, agg_t, part32, part16, rs_buf, pre_own, pre_all,
-    ext, picks, og_all, nb_pad, nb_send, nb_all, nb_nat, smat, grad_act, agg2, gscaled, gagg,
+    ext, picks, picks_t, og_all, nb1, nb_send, nb_all, nb_nat, smat, smat_t, grad_act, agg2, gscaled, gagg,
     halo_out, back_out, back_in, gtotal, gp, pair_out, pair_in, chip_buf,
     load_sem, rs_s, rs_r, ag_s, ag_r, og_s, og_r, nb_s, nb_r, halo_sem, back_sem,
     pa_s, pa_r, x_s, x_r, pb_s, pb_r,
@@ -71,7 +84,7 @@
     f, d = lax.axis_index("feat"), lax.axis_index("dp")
     src, width = face.shape
     targets, hid = nb1.shape[0], w1.shape[1]
-    own = nb2.shape[0]
+    own = og.shape[0]
     halo = srows.shape[1]
     full = targets + halo
     mine = pl.ds(pl.multiple_of(f * own, own), own)
@@ -95,9 +108,8 @@
     for i in range(1, parts):
         pl.semaphore_signal(barrier, inc=1, device_id={"dp": lax.rem(d + i, parts)}, device_id_type=MESH)
 
-    nb_pad[...] = jnp.full(nb_pad.shape, -1.0, F32)
-    nb_pad[:own, :8] = nb2[...].astype(F32)
-    nb_send[...] = jnp.transpose(nb_pad[...])[:8]
+    nb_send[...] = jnp.full(nb_send.shape, -1.0, F32)
+    nb_send[:, :own] = live(nb2_t[...], count2[...])
     if nb_all.shape[0] > n * 8:
         nb_all[n * 8 :, :] = jnp.full((nb_all.shape[0] - n * 8, 128), -1.0, F32)
     nb_all[pl.ds(pl.multiple_of(f * 8, 8), 8), :] = nb_send[...]
@@ -105,25 +117,64 @@
     picks[...] = jnp.where(
         lax.broadcasted_iota(jnp.int32, (targets, halo), 0) == srows[...], 1.0, 0.0
     ).astype(BF16)
+    names = live(nb1_t[...], count1[...])
+    for at in range(0, targets, 128):
+        tile = jnp.concatenate([names[:, at : at + 128], jnp.zeros((120, 128), F32)], axis=0)
+        nb1[at : at + 128, :] = jnp.transpose(tile)
 
     pl.semaphore_wait(barrier, n - 1 + parts - 1)
 
-    def gathered(source, buffer, rows, sends, recvs):
-        place = buffer.at[pl.ds(pl.multiple_of(f * rows, rows), rows)]
-        copies = []
-        for i in range(1, n):
-            copies.append(
-                pltpu.make_async_remote_copy(
-                    source, place, sends.at[i], recvs.at[i],
-                    device_id={"feat": lax.rem(f + i, n)}, device_id_type=MESH,
+    pair = f + 1 - 2 * lax.rem(f, 2)
+    outer = n // 2
+
+    def held(buffer, owner):
+        return buffer.at[pl.ds(pl.multiple_of(owner * own, own), own)]
+
+    def gather(source, buffer, sends, recvs):
+        first_hop = [
+            pltpu.make_async_remote_copy(
+                source, held(buffer, f), sends.at[0, i], recvs.at[0, i],
+                device_id={"feat": lax.rem(f + 2 * i, n)}, device_id_type=MESH,
+            )
+            for i in range(1, outer)
+        ]
+        to_mate = [
+            pltpu.make_async_remote_copy(
+                source, held(buffer, f), sends.at[1, 0], recvs.at[1, 0],
+                device_id={"feat": pair}, device_id_type=MESH,
+            )
+        ]
+        for copy in first_hop + to_mate:
+            copy.start()
+
+        def onward():
+            for i in range(1, outer):
+                first_hop[i - 1].wait_recv()
+                owner = held(buffer, lax.rem(f + n - 2 * i, n))
+                copy = pltpu.make_async_remote_copy(
+                    owner, owner, sends.at[1, i], recvs.at[1, i],
+                    device_id={"feat": pair}, device_id_type=MESH,
                 )
-            )
-        for copy in copies:
-            copy.start()
-        return copies
-
-    nb_copies = gathered(nb_send, nb_all, 8, nb_s, nb_r)
-    og_copies = gathered(og, og_all, own, og_s, og_r)
+                copy.start()
+                to_mate.append(copy)
+
+        def finish():
+            for copy in first_hop:
+                copy.wait_send()
+            for copy in to_mate:
+                copy.wait()
+
+        return onward, finish
+
+    nb_copies = []
+    for i in range(1, n):
+        copy = pltpu.make_async_remote_copy(
+            nb_send, nb_all.at[pl.ds(pl.multiple_of(f * 8, 8), 8)], nb_s.at[i], nb_r.at[i],
+            device_id={"feat": lax.rem(f + i, n)}, device_id_type=MESH,
+        )
+        copy.start()
+        nb_copies.append(copy)
+    og_onward, og_finish = gather(og, og_all, og_s, og_r)
 
     blocks = targets // block
     per = block // own
@@ -143,7 +194,7 @@
         at = pl.multiple_of(lax.rem(first + i, blocks) * block, block)
         rows = pl.ds(at, block)
         counts_matrix(nb1, at, adj, 0, block, src)
-        inv = inverse(nb1[rows, :])
+        inv = inverse(nb1[rows, :8])
         total = jnp.zeros((block, hid), F32)
         for j, (lane, size) in enumerate(cols):
             if blocks <= 2 and i == 0:
@@ -161,10 +212,15 @@
             dest = lax.rem(first + i, blocks) * per + j
             pl.when(dest != f)(lambda dest=dest: send_to(dest).start())
 
-    steps(blocks, first_layer)
-
-    for lane, size in cols:
-        agg_t[lane : lane + size, :] = jnp.transpose(agg[:, lane : lane + size])
+    if blocks <= 2:
+        first_layer(0)
+        og_onward()
+        for i in range(1, blocks):
+            first_layer(i)
+    else:
+        pl.loop(0, blocks)(first_layer)
+        og_onward()
+
     for copy in nb_copies:
         copy.wait()
     for at in range(0, nb_all.shape[0], 128):
@@ -173,14 +229,7 @@
             t = at // 8 + j
             nb_nat[t * own : (t + 1) * own, :8] = turned[:own, j * 8 : j * 8 + 8]
     counts_matrix(nb_nat, 0, smat, 0, targets, full)
-    for copy in late + og_copies:
-        copy.wait()
-
-    def out_part(i):
-        rows = pl.ds(pl.multiple_of(i * block, block), block)
-        grad_act[rows, :] = dot_last(og_all[rows, :], wout[...])
-
-    steps(blocks, out_part)
+    picks_t[...] = jnp.transpose(picks[...])
 
     value = part32[mine, :] + b1[...]
     for i in range(1, n):
@@ -192,11 +241,32 @@
         value = value + rs_buf[source].astype(F32)
     pre_own[...] = value.astype(BF16)
     pre_all[mine, :] = value.astype(BF16)
-    for copy in gathered(pre_own, pre_all, own, ag_s, ag_r):
+    onward, finish = gather(pre_own, pre_all, ag_s, ag_r)
+
+    for copy in late:
         copy.wait()
-
-    ext[:targets, :] = jax.nn.silu(pre_all[...].astype(F32)).astype(BF16)
-    halo_out[...] = dot_first(picks[...], ext[:targets, :]).astype(BF16)
+    og_finish()
+
+    def out_part(i):
+        rows = pl.ds(pl.multiple_of(i * block, block), block)
+        grad_act[rows if blocks <= 2 else slice(None), :] = dot_last(og_all[rows, :], wout[...])
+
+    if blocks <= 2:
+        steps(blocks, out_part)
+    for lane, size in split(full, 128):
+        smat_t[lane : lane + size, :] = jnp.transpose(smat[:, lane : lane + size])
+    onward()
+    for lane, size in cols:
+        agg_t[lane : lane + size, :] = jnp.transpose(agg[:, lane : lane + size])
+    finish()
+
+    def hidden_part(i):
+        rows = pl.ds(pl.multiple_of(i * block, block), block)
+        value = pre_all[rows, :].astype(F32)
+        ext[rows, :] = (value * sigmoid(value)).astype(BF16)
+
+    steps(blocks, hidden_part)
+    halo_out[...] = dot(picks_t[...], ext[:targets, :]).astype(BF16)
     halo_copy = pltpu.make_async_remote_copy(
         halo_out, ext.at[pl.ds(targets, halo)], halo_sem.at[0], halo_sem.at[1],
         device_id={"dp": lax.rem(d + 1, parts)}, device_id_type=MESH,
@@ -213,17 +283,19 @@
     def second_layer(i):
         rows = pl.ds(pl.multiple_of(i * block, block), block)
         inv = inverse(nb_nat[rows, :8])
+        if blocks > 2:
+            out_part(i)
         total = gagg[rows, :] + dot(smat[rows, targets:], ext[targets:, :])
         value = (ext[rows, :].astype(F32) + total * inv).astype(BF16)
         agg2[rows, :] = value
-        step = (grad_act[rows, :] * slope(dot(value, win[...]))).astype(BF16)
+        step = (grad_act[rows if blocks <= 2 else slice(None), :] * slope(dot(value, win[...]))).astype(BF16)
         back = dot_last(step, win[...])
         gagg[rows, :] = back
         gscaled[rows, :] = (back * inv).astype(BF16)
 
     steps(blocks, second_layer)
 
-    back_out[...] = dot_first(smat[:, targets:], gscaled[...]).astype(BF16)
+    back_out[...] = dot(smat_t[targets:, :], gscaled[...]).astype(BF16)
     back_copy = pltpu.make_async_remote_copy(
         back_out, back_in, back_sem.at[0], back_sem.at[1],
         device_id={"dp": lax.rem(d + parts - 1, parts)}, device_id_type=MESH,
@@ -233,15 +305,20 @@
     for at, size in split(targets, 512):
         rows = slice(at, at + size)
         gtotal[rows, :] = (
-            og_all[rows, :].astype(F32) + gagg[rows, :] + dot_first(smat[:, rows], gscaled[...])
+            og_all[rows, :].astype(F32) + gagg[rows, :] + dot(smat_t[rows, :], gscaled[...])
         )
-    act = jax.nn.silu(dot(agg2[mine, :], win[...])).astype(BF16)
+    value = dot(agg2[mine, :], win[...])
+    act = (value * sigmoid(value)).astype(BF16)
     embed[...] = (ext[mine, :].astype(F32) + dot(act, wout[...])).astype(BF16)
 
     back_copy.wait()
-    gp[...] = (
-        (gtotal[...] + dot(picks[...], back_in[...])) * slope(pre_all[...].astype(F32))
-    ).astype(BF16)
+
+    def first_gradient(i):
+        rows = pl.ds(pl.multiple_of(i * block, block), block)
+        value = gtotal[rows, :] + dot(picks[rows, :], back_in[...])
+        gp[rows, :] = (value * slope(pre_all[rows, :].astype(F32))).astype(BF16)
+
+    steps(blocks, first_gradient)
 
     half = width // 2
     size = half // chunks
@@ -296,11 +373,60 @@
         send_to(lax.rem(f + i, n)).wait_send()
 
 
-def fused(n, parts, face_grid, nb1, w_first, b_first, send_rows, nb2, w_in, w_out, out_grad):
+def finish_kernel(embed_in, grad_in, embed, grad, narrow, wide, in_sem, out_sem):
+    rows, pieces = grad_in.shape[0], in_sem.shape[0] - 1
+    size = rows // pieces
+    small = pltpu.make_async_copy(embed_in, embed, in_sem.at[pieces])
+    small.start()
+
+    def part(ref, i):
+        return ref.at[pl.ds(i * size, size)]
+
+    arrive = [
+        pltpu.make_async_copy(part(grad_in, i), part(narrow, i), in_sem.at[i]) for i in range(pieces)
+    ]
+    leave = [pltpu.make_async_copy(part(wide, i), part(grad, i), out_sem.at[i]) for i in range(pieces)]
+    for copy in arrive:
+        copy.start()
+    for i in range(pieces):
+        arrive[i].wait()
+        span = slice(i * size, (i + 1) * size)
+        wide[span, :] = narrow[span, :].astype(F32)
+        leave[i].start()
+    small.wait()
+    for copy in leave:
+        copy.wait()
+
+
+def finished(embed, grad):
+    pieces = next(c for c in (4, 2, 1) if (grad.shape[0] // c) % 16 == 0)
+    any_space = pl.BlockSpec(memory_space=pl.ANY)
+    return pl.pallas_call(
+        finish_kernel,
+        out_shape=(
+            jax.ShapeDtypeStruct(embed.shape, BF16),
+            jax.ShapeDtypeStruct(grad.shape, F32),
+        ),
+        in_specs=[any_space, any_space],
+        out_specs=(any_space, any_space),
+        scratch_shapes=[
+            pltpu.VMEM(grad.shape, BF16),
+            pltpu.VMEM(grad.shape, F32),
+            pltpu.SemaphoreType.DMA((pieces + 1,)),
+            pltpu.SemaphoreType.DMA((pieces,)),
+        ],
+        compiler_params=pltpu.CompilerParams(vmem_limit_bytes=56 * 1024 * 1024),
+        name="finish",
+    )(embed, grad)
+
+
+def fused(
+    n, parts, face_grid, nb1, count1, w_first, b_first, send_rows, nb2, count2, w_in, w_out, out_grad
+):
     src, width = face_grid.shape
-    targets, hid = nb1.shape[0], w_first.shape[1]
+    targets, hid = nb1.shape[1], w_first.shape[1]
     inner = w_in.shape[1]
-    own, halo = nb2.shape[0], send_rows.shape[1]
+    own, halo = nb2.shape[1], send_rows.shape[1]
     full = targets + halo
     block = min(targets, 256)
     half = width // 2
@@ -316,7 +442,9 @@
             jax.ShapeDtypeStruct((own, hid), BF16),
             jax.ShapeDtypeStruct((width, hid), BF16),
         ),
-        in_specs=[any_space, vmem, any_space, vmem, vmem, vmem, any_space, any_space, vmem],
+        in_specs=[
+            any_space, vmem, vmem, any_space, vmem, vmem, vmem, vmem, any_space, any_space, vmem,
+        ],
         out_specs=(vmem, vmem),
         scratch_shapes=[
             pltpu.VMEM((src, width), BF16),
@@ -333,13 +461,15 @@
             pltpu.VMEM((targets, hid), BF16),
             pltpu.VMEM((full, hid), BF16),
             pltpu.VMEM((targets, halo), BF16),
+            pltpu.VMEM((halo, targets), BF16),
             pltpu.VMEM((targets, hid), BF16),
-            pltpu.VMEM((128, 128), F32),
+            pltpu.VMEM((targets, 128), F32),
             pltpu.VMEM((8, 128), F32),
             pltpu.VMEM((tiles, 128), F32),
             pltpu.VMEM((targets, 128), F32),
             pltpu.VMEM((targets, full), BF16),
-            pltpu.VMEM((targets, inner), F32),
+            pltpu.VMEM((full, targets), BF16),
+            pltpu.VMEM((targets if targets // block <= 2 else block, inner), F32),
             pltpu.VMEM((targets, hid), BF16),
             pltpu.VMEM((targets, hid), BF16),
             pltpu.VMEM((targets, hid), F32),
@@ -352,25 +482,24 @@
             pltpu.VMEM((half, hid), BF16),
             pltpu.VMEM((chips, half, hid), BF16),
             dma((len(split(width, 256)) + 3,)),
-            dma((n,)), dma((n,)), dma((n,)), dma((n,)), dma((n,)), dma((n,)), dma((n,)), dma((n,)),
+            dma((n,)), dma((n,)),
+            dma((2, n // 2)), dma((2, n // 2)), dma((2, n // 2)), dma((2, n // 2)),
+            dma((n,)), dma((n,)),
             dma((2,)), dma((2,)),
             dma((chunks,)), dma((chunks,)),
             dma((chips, chunks)), dma((chips, chunks)),
             dma((chunks,)), dma((chunks,)),
         ],
         compiler_params=pltpu.CompilerParams(
-            collective_id=0, has_side_effects=True, vmem_limit_bytes=56 * 1024 * 1024
+            collective_id=0, has_side_effects=True, vmem_limit_bytes=60 * 1024 * 1024
         ),
         cost_estimate=pl.CostEstimate(
             flops=2 * targets * src * width, bytes_accessed=2 * src * width, transcendentals=0
         ),
         name="fused_step",
-    )(face_grid, nb1, w_first, b_first, send_rows, nb2, w_in, w_out, out_grad)
-
-
-def live(nbrs, count):
-    slots = jnp.arange(nbrs.shape[1], dtype=jnp.int32)
-    return jnp.where(slots[None, :] < count[:, None], nbrs, -1)
+    )(
+        face_grid, nb1, count1, w_first, b_first, send_rows, nb2, count2, w_in, w_out, out_grad
+    )
 
 
 def solution(mesh):
@@ -381,10 +510,11 @@
         second_nbrs, second_count, w_in, w_out, out_grad,
     ):
         embed, grad = fused(
-            n, parts, face_grid, live(first_nbrs, first_count), w_first, b_first.reshape(1, -1),
-            send_rows.reshape(1, -1), live(second_nbrs, second_count), w_in, w_out, out_grad,
+            n, parts, face_grid, first_nbrs.T, first_count.reshape(1, -1), w_first,
+            b_first.reshape(1, -1), send_rows.reshape(1, -1), second_nbrs.T,
+            second_count.reshape(1, -1), w_in, w_out, out_grad,
         )
-        return embed, grad.astype(F32)
+        return finished(embed, grad)
 
     return jax.shard_map(
         body,

time: 55.2 us -> 48.7 us (0.88)
  the two profiles are of different devices: /device:TPU:25 before, /device:TPU:0 now
where the time goes in v2:
time: 48.7 us; the launch traced here: 48.5 us
  Pallas kernels  47.8 us (98%)
  between operations  0.64 us (1%)
    pallas_call x1, Pallas kernels, fused(): pl.pallas_call(functools.partial(kernel, n, parts, block, chunks), out_sh...  45.6 us
    pallas_call x1, Pallas kernels, finished(): pl.pallas_call(finish_kernel, out_shape=(jax.ShapeDtypeStruct(embed.shape...  2.18 us

profile of v2, /device:TPU:0, one launch (start us, length us, event | category | flops | bytes accessed | tf_op | source)
XLA Modules:
  0.0 48.5 jit_solution(10705584692873837416)
XLA Ops:
  0.6 45.6 %fused_step.1 = (bf16[64,256]{1,0:T(8,128)(2,1)}, bf16[1280,256]{1,0:T(8,128)(2,1)}) custom-call(bf16[1024,1280]{1,0:T(8,128)(2,1)} %face_hbm.1, s32[8,512]{1,0:T(8,128)} %bitcast.6, s32[1,512]{1,0:T(1,128)} %bitcast.8, bf16[1280,256]{1,0:T(8,128)(2,1)} %w1_hbm.1, f32[1,256]{1,0:T(1,128)} %bitcast.9, s32[1,128]{1,0:T(1,128)} %bitcast.10, s32[8,64]{1,0:T(8,128)} %bitcast.7, ...), custom_call_target="tpu_custom_call" | custom-call | flops 1342177280 | bytes 2621440 | tf_op jit(solution)/shard_map/fused_step/pallas_call | solution.py:439
  46.3 2.2 %finish.1 = (bf16[64,256]{1,0:T(8,128)(2,1)}, f32[1280,256]{1,0:T(8,128)}) custom-call(bf16[64,256]{1,0:T(8,128)(2,1)} %get-tuple-element.4.embed_in, bf16[1280,256]{1,0:T(8,128)(2,1)} %get-tuple-element.5.grad_in), custom_call_target="tpu_custom_call" | custom-call | tf_op jit(solution)/shard_map/finish/pallas_call | solution.py:404

commit v3 on v2

--- a/solution.py
+++ b/solution.py
@@ -58,7 +58,13 @@
             here = pl.ds(pl.multiple_of(at + g * 16, 16), 16)
             out[here, lane : lane + size] = jnp.concatenate(pieces, axis=0).astype(BF16)
 
-    pl.loop(0, rows // 16)(group)
+    several = 4 if width <= 1024 and rows % 64 == 0 else 1
+
+    def groups(i):
+        for j in range(several):
+            group(i * several + j)
+
+    pl.loop(0, rows // 16 // several)(groups)
 
 
 def live(nbrs, count):
@@ -122,6 +128,11 @@
         tile = jnp.concatenate([names[:, at : at + 128], jnp.zeros((120, 128), F32)], axis=0)
         nb1[at : at + 128, :] = jnp.transpose(tile)
 
+    blocks = targets // block
+    per = block // own
+    first = lax.rem(f // per + 1, blocks)
+    counts_matrix(nb1, pl.multiple_of(first * block, block), adj, 0, block, src)
+
     pl.semaphore_wait(barrier, n - 1 + parts - 1)
 
     pair = f + 1 - 2 * lax.rem(f, 2)
@@ -176,10 +187,6 @@
         nb_copies.append(copy)
     og_onward, og_finish = gather(og, og_all, og_s, og_r)
 
-    blocks = targets // block
-    per = block // own
-    first = lax.rem(f // per + 1, blocks)
-
     def send_to(dest):
         return pltpu.make_async_remote_copy(
             part16.at[pl.ds(pl.multiple_of(dest * own, own), own)], rs_buf.at[f],
@@ -193,7 +200,10 @@
     def first_layer(i):
         at = pl.multiple_of(lax.rem(first + i, blocks) * block, block)
         rows = pl.ds(at, block)
-        counts_matrix(nb1, at, adj, 0, block, src)
+        if not isinstance(i, int):
+            pl.when(i > 0)(lambda: counts_matrix(nb1, at, adj, 0, block, src))
+        elif i > 0:
+            counts_matrix(nb1, at, adj, 0, block, src)
         inv = inverse(nb1[rows, :8])
         total = jnp.zeros((block, hid), F32)
         for j, (lane, size) in enumerate(cols):
@@ -230,6 +240,18 @@
             nb_nat[t * own : (t + 1) * own, :8] = turned[:own, j * 8 : j * 8 + 8]
     counts_matrix(nb_nat, 0, smat, 0, targets, full)
     picks_t[...] = jnp.transpose(picks[...])
+    for copy in late:
+        copy.wait()
+    og_finish()
+
+    def out_part(i):
+        rows = pl.ds(pl.multiple_of(i * block, block), block)
+        grad_act[rows if blocks <= 2 else slice(None), :] = dot_last(og_all[rows, :], wout[...])
+
+    if blocks <= 2:
+        steps(blocks, out_part)
+    for lane, size in split(full, 128):
+        smat_t[lane : lane + size, :] = jnp.transpose(smat[:, lane : lane + size])
 
     value = part32[mine, :] + b1[...]
     for i in range(1, n):
@@ -243,20 +265,9 @@
     pre_all[mine, :] = value.astype(BF16)
     onward, finish = gather(pre_own, pre_all, ag_s, ag_r)
 
-    for copy in late:
-        copy.wait()
-    og_finish()
-
-    def out_part(i):
-        rows = pl.ds(pl.multiple_of(i * block, block), block)
-        grad_act[rows if blocks <= 2 else slice(None), :] = dot_last(og_all[rows, :], wout[...])
-
-    if blocks <= 2:
-        steps(blocks, out_part)
-    for lane, size in split(full, 128):
-        smat_t[lane : lane + size, :] = jnp.transpose(smat[:, lane : lane + size])
     onward()
-    for lane, size in cols:
+    early = (len(cols) + 1) // 2
+    for lane, size in cols[:early]:
         agg_t[lane : lane + size, :] = jnp.transpose(agg[:, lane : lane + size])
     finish()
 
@@ -278,6 +289,8 @@
         gagg[rows, :] = dot(smat[rows, :targets], ext[:targets, :])
 
     steps(blocks, neighbour_part)
+    for lane, size in cols[early:]:
+        agg_t[lane : lane + size, :] = jnp.transpose(agg[:, lane : lane + size])
     halo_copy.wait()
 
     def second_layer(i):

time: 48.7 us -> 50.8 us (1.043)
  Pallas kernels: 47.8 us -> 49.9 us
    pallas_call x1, Pallas kernels: 45.6 us -> 47.7 us  [fused(): pl.pallas_call(functools.partial(kernel, n, parts, block, chunks), out_sh...]
where the time goes in v3:
time: 50.8 us; the launch traced here: 50.6 us
  Pallas kernels  49.9 us (98%)
  between operations  0.64 us (1%)
    pallas_call x1, Pallas kernels, fused(): pl.pallas_call(functools.partial(kernel, n, parts, block, chunks), out_sh...  47.7 us
    pallas_call x1, Pallas kernels, finished(): pl.pallas_call(finish_kernel, out_shape=(jax.ShapeDtypeStruct(embed.shape...  2.18 us

profile of v3, /device:TPU:0, one launch (start us, length us, event | category | flops | bytes accessed | tf_op | source)
XLA Modules:
  0.0 50.6 jit_solution(16866047530334803632)
XLA Ops:
  0.6 47.7 %fused_step.1 = (bf16[64,256]{1,0:T(8,128)(2,1)}, bf16[1280,256]{1,0:T(8,128)(2,1)}) custom-call(bf16[1024,1280]{1,0:T(8,128)(2,1)} %face_hbm.1, s32[8,512]{1,0:T(8,128)} %bitcast.6, s32[1,512]{1,0:T(1,128)} %bitcast.8, bf16[1280,256]{1,0:T(8,128)(2,1)} %w1_hbm.1, f32[1,256]{1,0:T(1,128)} %bitcast.9, s32[1,128]{1,0:T(1,128)} %bitcast.10, s32[8,64]{1,0:T(8,128)} %bitcast.7, ...), custom_call_target="tpu_custom_call" | custom-call | flops 1342177280 | bytes 2621440 | tf_op jit(solution)/shard_map/fused_step/pallas_call | solution.py:452
  48.4 2.2 %finish.1 = (bf16[64,256]{1,0:T(8,128)(2,1)}, f32[1280,256]{1,0:T(8,128)}) custom-call(bf16[64,256]{1,0:T(8,128)(2,1)} %get-tuple-element.4.embed_in, bf16[1280,256]{1,0:T(8,128)(2,1)} %get-tuple-element.5.grad_in), custom_call_target="tpu_custom_call" | custom-call | tf_op jit(solution)/shard_map/finish/pallas_call | solution.py:417

commit v4 on v3

--- a/solution.py
+++ b/solution.py
@@ -223,13 +223,11 @@
             pl.when(dest != f)(lambda dest=dest: send_to(dest).start())
 
     if blocks <= 2:
-        first_layer(0)
-        og_onward()
-        for i in range(1, blocks):
+        for i in range(blocks):
             first_layer(i)
     else:
         pl.loop(0, blocks)(first_layer)
-        og_onward()
+    og_onward()
 
     for copy in nb_copies:
         copy.wait()
@@ -240,16 +238,6 @@
             nb_nat[t * own : (t + 1) * own, :8] = turned[:own, j * 8 : j * 8 + 8]
     counts_matrix(nb_nat, 0, smat, 0, targets, full)
     picks_t[...] = jnp.transpose(picks[...])
-    for copy in late:
-        copy.wait()
-    og_finish()
-
-    def out_part(i):
-        rows = pl.ds(pl.multiple_of(i * block, block), block)
-        grad_act[rows if blocks <= 2 else slice(None), :] = dot_last(og_all[rows, :], wout[...])
-
-    if blocks <= 2:
-        steps(blocks, out_part)
     for lane, size in split(full, 128):
         smat_t[lane : lane + size, :] = jnp.transpose(smat[:, lane : lane + size])
 
@@ -264,6 +252,16 @@
     pre_own[...] = value.astype(BF16)
     pre_all[mine, :] = value.astype(BF16)
     onward, finish = gather(pre_own, pre_all, ag_s, ag_r)
+    for copy in late:
+        copy.wait()
+    og_finish()
+
+    def out_part(i):
+        rows = pl.ds(pl.multiple_of(i * block, block), block)
+        grad_act[rows if blocks <= 2 else slice(None), :] = dot_last(og_all[rows, :], wout[...])
+
+    if blocks <= 2:
+        steps(blocks, out_part)
 
     onward()
     early = (len(cols) + 1) // 2

time: 50.8 us -> 48.6 us (0.957)
  Pallas kernels: 49.9 us -> 47.8 us
    pallas_call x1, Pallas kernels: 47.7 us -> 45.6 us  [fused(): pl.pallas_call(functools.partial(kernel, n, parts, block, chunks), out_sh...]
where the time goes in v4:
time: 48.6 us; the launch traced here: 48.4 us
  Pallas kernels  47.8 us (98%)
  between operations  0.64 us (1%)
    pallas_call x1, Pallas kernels, fused(): pl.pallas_call(functools.partial(kernel, n, parts, block, chunks), out_sh...  45.6 us
    pallas_call x1, Pallas kernels, finished(): pl.pallas_call(finish_kernel, out_shape=(jax.ShapeDtypeStruct(embed.shape...  2.18 us

profile of v4, /device:TPU:0, one launch (start us, length us, event | category | flops | bytes accessed | tf_op | source)
XLA Modules:
  0.0 48.4 jit_solution(5353681228380205380)
XLA Ops:
  0.6 45.6 %fused_step.1 = (bf16[64,256]{1,0:T(8,128)(2,1)}, bf16[1280,256]{1,0:T(8,128)(2,1)}) custom-call(bf16[1024,1280]{1,0:T(8,128)(2,1)} %face_hbm.1, s32[8,512]{1,0:T(8,128)} %bitcast.6, s32[1,512]{1,0:T(1,128)} %bitcast.8, bf16[1280,256]{1,0:T(8,128)(2,1)} %w1_hbm.1, f32[1,256]{1,0:T(1,128)} %bitcast.9, s32[1,128]{1,0:T(1,128)} %bitcast.10, s32[8,64]{1,0:T(8,128)} %bitcast.7, ...), custom_call_target="tpu_custom_call" | custom-call | flops 1342177280 | bytes 2621440 | tf_op jit(solution)/shard_map/fused_step/pallas_call | solution.py:450
  46.2 2.2 %finish.1 = (bf16[64,256]{1,0:T(8,128)(2,1)}, f32[1280,256]{1,0:T(8,128)}) custom-call(bf16[64,256]{1,0:T(8,128)(2,1)} %get-tuple-element.4.embed_in, bf16[1280,256]{1,0:T(8,128)(2,1)} %get-tuple-element.5.grad_in), custom_call_target="tpu_custom_call" | custom-call | tf_op jit(solution)/shard_map/finish/pallas_call | solution.py:415

commit v5 on v4

--- a/solution.py
+++ b/solution.py
@@ -29,7 +29,7 @@
 
 
 def steps(count, fn):
-    if count <= 2:
+    if count <= 1:
         for i in range(count):
             fn(i)
     else:
@@ -81,10 +81,10 @@
     n, parts, block, chunks,
     face_hbm, nb1_t, count1, w1_hbm, b1, srows, nb2_t, count2, win_hbm, wout_hbm, og,
     embed, grad,
-    face, w1, win, wout, adj, agg, agg_t, part32, part16, rs_buf, pre_own, pre_all,
+    face, w1, win, wout, adj, agg, agg_t, part32, part16, pair_buf, sums, pre_sum, rs_buf, pre_own, pre_all,
     ext, picks, picks_t, og_all, nb1, nb_send, nb_all, nb_nat, smat, smat_t, grad_act, agg2, gscaled, gagg,
     halo_out, back_out, back_in, gtotal, gp, pair_out, pair_in, chip_buf,
-    load_sem, rs_s, rs_r, ag_s, ag_r, og_s, og_r, nb_s, nb_r, halo_sem, back_sem,
+    load_sem, pr_s, pr_r, rs_s, rs_r, ag_s, ag_r, og_s, og_r, nb_s, nb_r, halo_sem, back_sem,
     pa_s, pa_r, x_s, x_r, pb_s, pb_r,
 ):
     f, d = lax.axis_index("feat"), lax.axis_index("dp")
@@ -187,46 +187,69 @@
         nb_copies.append(copy)
     og_onward, og_finish = gather(og, og_all, og_s, og_r)
 
-    def send_to(dest):
+    column, parity = f // 2, lax.rem(f, 2)
+
+    def to_pair(other):
+        there = pl.ds(pl.multiple_of((2 * other + 1 - parity) * own, own), own)
         return pltpu.make_async_remote_copy(
-            part16.at[pl.ds(pl.multiple_of(dest * own, own), own)], rs_buf.at[f],
-            rs_s.at[dest], rs_r.at[f], device_id={"feat": dest}, device_id_type=MESH,
-        )
-
-    if blocks > 2:
-        for copy in loads:
-            copy.wait()
+            part16.at[there], pair_buf.at[other], pr_s.at[other], pr_r.at[other],
+            device_id={"feat": pair}, device_id_type=MESH,
+        )
+
+    def to_owner(other):
+        return pltpu.make_async_remote_copy(
+            sums.at[other], rs_buf.at[column], rs_s.at[other], rs_r.at[column],
+            device_id={"feat": 2 * other + parity}, device_id_type=MESH,
+        )
+
+    def by_columns(fn, first_col, last_col):
+        if width % 256 == 0:
+            pl.loop(first_col, last_col)(lambda j: fn(pl.multiple_of(j * 256, 256), 256))
+        else:
+            for lane, size in cols[first_col:last_col]:
+                fn(lane, size)
+
+    for copy in loads:
+        copy.wait()
 
     def first_layer(i):
-        at = pl.multiple_of(lax.rem(first + i, blocks) * block, block)
+        which = lax.rem(first + i, blocks)
+        at = pl.multiple_of(which * block, block)
         rows = pl.ds(at, block)
-        if not isinstance(i, int):
+        if blocks > 1:
             pl.when(i > 0)(lambda: counts_matrix(nb1, at, adj, 0, block, src))
-        elif i > 0:
-            counts_matrix(nb1, at, adj, 0, block, src)
         inv = inverse(nb1[rows, :8])
-        total = jnp.zeros((block, hid), F32)
-        for j, (lane, size) in enumerate(cols):
-            if blocks <= 2 and i == 0:
-                loads[j].wait()
-                if j == 0:
-                    loads[-1].wait()
-            chunk = slice(lane, lane + size)
+        part32[rows, :] = jnp.zeros((block, hid), F32)
+
+        def column_part(lane, size):
+            chunk = pl.ds(lane, size)
             value = dot(adj[...], face[:, chunk]) * inv + face[rows, chunk].astype(F32)
             value = value.astype(BF16)
             agg[rows, chunk] = value
-            total = total + dot(value, w1[chunk, :])
-        part32[rows, :] = total
-        part16[rows, :] = total.astype(BF16)
-        for j in range(per):
-            dest = lax.rem(first + i, blocks) * per + j
-            pl.when(dest != f)(lambda dest=dest: send_to(dest).start())
-
-    if blocks <= 2:
-        for i in range(blocks):
-            first_layer(i)
-    else:
-        pl.loop(0, blocks)(first_layer)
+            part32[rows, :] += dot(value, w1[chunk, :])
+
+        by_columns(column_part, 0, len(cols))
+        part16[rows, :] = part32[rows, :].astype(BF16)
+        for j in range(per // 2):
+            to_pair(which * (per // 2) + j).start()
+
+    steps(blocks, first_layer)
+
+    side_size = outer // 2
+    side_at = column // side_size * side_size
+    far_at = (outer - side_size) - side_at
+    far = [far_at + lax.rem(column + i, side_size) for i in range(side_size)]
+    near = [side_at + lax.rem(column + i, side_size) for i in range(1, side_size)]
+
+    def pair_sum(other):
+        to_pair(other).wait_recv()
+        rows = pl.ds(pl.multiple_of((2 * other + parity) * own, own), own)
+        return part32[rows, :] + pair_buf[other].astype(F32)
+
+    for other in far + near:
+        sums[other] = pair_sum(other).astype(BF16)
+        to_owner(other).start()
+    pre_sum[...] = pair_sum(column) + b1[...]
     og_onward()
 
     for copy in nb_copies:
@@ -238,17 +261,20 @@
             nb_nat[t * own : (t + 1) * own, :8] = turned[:own, j * 8 : j * 8 + 8]
     counts_matrix(nb_nat, 0, smat, 0, targets, full)
     picks_t[...] = jnp.transpose(picks[...])
-    for lane, size in split(full, 128):
-        smat_t[lane : lane + size, :] = jnp.transpose(smat[:, lane : lane + size])
-
-    value = part32[mine, :] + b1[...]
-    for i in range(1, n):
-        source = lax.rem(f + i, n)
+
+    def turn_smat(j):
+        lane = pl.ds(pl.multiple_of(j * 128, 128), 128)
+        smat_t[lane, :] = jnp.transpose(smat[:, lane])
+
+    pl.loop(0, full // 128)(turn_smat)
+
+    value = pre_sum[...]
+    for other in far + near:
         pltpu.make_async_remote_copy(
-            part16.at[pl.ds(0, own)], rs_buf.at[source], rs_s.at[source], rs_r.at[source],
-            device_id={"feat": source}, device_id_type=MESH,
+            sums.at[other], rs_buf.at[other], rs_s.at[other], rs_r.at[other],
+            device_id={"feat": 2 * other + parity}, device_id_type=MESH,
         ).wait_recv()
-        value = value + rs_buf[source].astype(F32)
+        value = value + rs_buf[other].astype(F32)
     pre_own[...] = value.astype(BF16)
     pre_all[mine, :] = value.astype(BF16)
     onward, finish = gather(pre_own, pre_all, ag_s, ag_r)
@@ -265,8 +291,11 @@
 
     onward()
     early = (len(cols) + 1) // 2
-    for lane, size in cols[:early]:
-        agg_t[lane : lane + size, :] = jnp.transpose(agg[:, lane : lane + size])
+
+    def turn_agg(lane, size):
+        agg_t[pl.ds(lane, size), :] = jnp.transpose(agg[:, pl.ds(lane, size)])
+
+    by_columns(turn_agg, 0, early)
     finish()
 
     def hidden_part(i):
@@ -287,8 +316,7 @@
         gagg[rows, :] = dot(smat[rows, :targets], ext[:targets, :])
 
     steps(blocks, neighbour_part)
-    for lane, size in cols[early:]:
-        agg_t[lane : lane + size, :] = jnp.transpose(agg[:, lane : lane + size])
+    by_columns(turn_agg, early, len(cols))
     halo_copy.wait()
 
     def second_layer(i):
@@ -380,8 +408,10 @@
         end_copies.append(copy)
     for copy in end_copies:
         copy.wait()
-    for i in range(1, n):
-        send_to(lax.rem(f + i, n)).wait_send()
+    for other in range(outer):
+        to_pair(other).wait_send()
+    for other in far + near:
+        to_owner(other).wait_send()
 
 
 def finish_kernel(embed_in, grad_in, embed, grad, narrow, wide, in_sem, out_sem):
@@ -467,7 +497,10 @@
             pltpu.VMEM((width, targets), BF16),
             pltpu.VMEM((targets, hid), F32),
             pltpu.VMEM((targets, hid), BF16),
-            pltpu.VMEM((n, own, hid), BF16),
+            pltpu.VMEM((n // 2, own, hid), BF16),
+            pltpu.VMEM((n // 2, own, hid), BF16),
+            pltpu.VMEM((own, hid), F32),
+            pltpu.VMEM((n // 2, own, hid), BF16),
             pltpu.VMEM((own, hid), BF16),
             pltpu.VMEM((targets, hid), BF16),
             pltpu.VMEM((full, hid), BF16),
@@ -493,7 +526,7 @@
             pltpu.VMEM((half, hid), BF16),
             pltpu.VMEM((chips, half, hid), BF16),
             dma((len(split(width, 256)) + 3,)),
-            dma((n,)), dma((n,)),
+            dma((n // 2,)), dma((n // 2,)), dma((n // 2,)), dma((n // 2,)),
             dma((2, n // 2)), dma((2, n // 2)), dma((2, n // 2)), dma((2, n // 2)),
             dma((n,)), dma((n,)),
             dma((2,)), dma((2,)),

time: 48.6 us -> 48.2 us (level)
  no operation moved by 1% of the time
where the time goes in v5:
time: 48.2 us; the launch traced here: 48 us
  Pallas kernels  47.4 us (98%)
  between operations  0.64 us (1%)
    pallas_call x1, Pallas kernels, fused(): pl.pallas_call(functools.partial(kernel, n, parts, block, chunks), out_sh...  45.2 us
    pallas_call x1, Pallas kernels, finished(): pl.pallas_call(finish_kernel, out_shape=(jax.ShapeDtypeStruct(embed.shape...  2.18 us

profile of v5, /device:TPU:0, one launch (start us, length us, event | category | flops | bytes accessed | tf_op | source)
XLA Modules:
  0.0 48.0 jit_solution(16173438337959068931)
XLA Ops:
  0.6 45.2 %fused_step.1 = (bf16[64,256]{1,0:T(8,128)(2,1)}, bf16[1280,256]{1,0:T(8,128)(2,1)}) custom-call(bf16[1024,1280]{1,0:T(8,128)(2,1)} %face_hbm.1, s32[8,512]{1,0:T(8,128)} %bitcast.6, s32[1,512]{1,0:T(1,128)} %bitcast.8, bf16[1280,256]{1,0:T(8,128)(2,1)} %w1_hbm.1, f32[1,256]{1,0:T(1,128)} %bitcast.9, s32[1,128]{1,0:T(1,128)} %bitcast.10, s32[8,64]{1,0:T(8,128)} %bitcast.7, ...), custom_call_target="tpu_custom_call" | custom-call | flops 1342177280 | bytes 2621440 | tf_op jit(solution)/shard_map/fused_step/pallas_call | solution.py:480
  45.8 2.2 %finish.1 = (bf16[64,256]{1,0:T(8,128)(2,1)}, f32[1280,256]{1,0:T(8,128)}) custom-call(bf16[64,256]{1,0:T(8,128)(2,1)} %get-tuple-element.4.embed_in, bf16[1280,256]{1,0:T(8,128)(2,1)} %get-tuple-element.5.grad_in), custom_call_target="tpu_custom_call" | custom-call | tf_op jit(solution)/shard_map/finish/pallas_call | solution.py:445

commit v6 on v5

--- a/solution.py
+++ b/solution.py
@@ -83,7 +83,7 @@
     embed, grad,
     face, w1, win, wout, adj, agg, agg_t, part32, part16, pair_buf, sums, pre_sum, rs_buf, pre_own, pre_all,
     ext, picks, picks_t, og_all, nb1, nb_send, nb_all, nb_nat, smat, smat_t, grad_act, agg2, gscaled, gagg,
-    halo_out, back_out, back_in, gtotal, gp, pair_out, pair_in, chip_buf,
+    halo_out, back_out, back_in, gtotal, gp, pair_out, pair_in, chip_buf, eye,
     load_sem, pr_s, pr_r, rs_s, rs_r, ag_s, ag_r, og_s, og_r, nb_s, nb_r, halo_sem, back_sem,
     pa_s, pa_r, x_s, x_r, pb_s, pb_r,
 ):
@@ -131,6 +131,10 @@
     blocks = targets // block
     per = block // own
     first = lax.rem(f // per + 1, blocks)
+    square = (256, 256)
+    eye[...] = jnp.where(
+        lax.broadcasted_iota(jnp.int32, square, 0) == lax.broadcasted_iota(jnp.int32, square, 1), 1.0, 0.0
+    ).astype(BF16)
     counts_matrix(nb1, pl.multiple_of(first * block, block), adj, 0, block, src)
 
     pl.semaphore_wait(barrier, n - 1 + parts - 1)
@@ -264,7 +268,7 @@
 
     def turn_smat(j):
         lane = pl.ds(pl.multiple_of(j * 128, 128), 128)
-        smat_t[lane, :] = jnp.transpose(smat[:, lane])
+        smat_t[lane, :] = dot_last(eye[:128, :128], smat[:, lane]).astype(BF16)
 
     pl.loop(0, full // 128)(turn_smat)
 
@@ -293,7 +297,7 @@
     early = (len(cols) + 1) // 2
 
     def turn_agg(lane, size):
-        agg_t[pl.ds(lane, size), :] = jnp.transpose(agg[:, pl.ds(lane, size)])
+        agg_t[pl.ds(lane, size), :] = dot_last(eye[:size, :size], agg[:, pl.ds(lane, size)]).astype(BF16)
 
     by_columns(turn_agg, 0, early)
     finish()
@@ -525,6 +529,7 @@
             pltpu.VMEM((half, hid), BF16),
             pltpu.VMEM((half, hid), BF16),
             pltpu.VMEM((chips, half, hid), BF16),
+            pltpu.VMEM((256, 256), BF16),
             dma((len(split(width, 256)) + 3,)),
             dma((n // 2,)), dma((n // 2,)), dma((n // 2,)), dma((n // 2,)),
             dma((2, n // 2)), dma((2, n // 2)), dma((2, n // 2)), dma((2, n // 2)),

time: 48.2 us -> 48.3 us (level)
  no operation moved by 1% of the time
where the time goes in v6:
time: 48.3 us; the launch traced here: 48.1 us
  Pallas kernels  47.5 us (98%)
  between operations  0.64 us (1%)
    pallas_call x1, Pallas kernels, fused(): pl.pallas_call(functools.partial(kernel, n, parts, block, chunks), out_sh...  45.3 us
    pallas_call x1, Pallas kernels, finished(): pl.pallas_call(finish_kernel, out_shape=(jax.ShapeDtypeStruct(embed.shape...  2.18 us

profile of v6, /device:TPU:0, one launch (start us, length us, event | category | flops | bytes accessed | tf_op | source)
XLA Modules:
  0.0 48.1 jit_solution(12508010552656793861)
XLA Ops:
  0.6 45.3 %fused_step.1 = (bf16[64,256]{1,0:T(8,128)(2,1)}, bf16[1280,256]{1,0:T(8,128)(2,1)}) custom-call(bf16[1024,1280]{1,0:T(8,128)(2,1)} %face_hbm.1, s32[8,512]{1,0:T(8,128)} %bitcast.6, s32[1,512]{1,0:T(1,128)} %bitcast.8, bf16[1280,256]{1,0:T(8,128)(2,1)} %w1_hbm.1, f32[1,256]{1,0:T(1,128)} %bitcast.9, s32[1,128]{1,0:T(1,128)} %bitcast.10, s32[8,64]{1,0:T(8,128)} %bitcast.7, ...), custom_call_target="tpu_custom_call" | custom-call | flops 1342177280 | bytes 2621440 | tf_op jit(solution)/shard_map/fused_step/pallas_call | solution.py:484
  45.9 2.2 %finish.1 = (bf16[64,256]{1,0:T(8,128)(2,1)}, f32[1280,256]{1,0:T(8,128)}) custom-call(bf16[64,256]{1,0:T(8,128)(2,1)} %get-tuple-element.4.embed_in, bf16[1280,256]{1,0:T(8,128)(2,1)} %get-tuple-element.5.grad_in), custom_call_target="tpu_custom_call" | custom-call | tf_op jit(solution)/shard_map/finish/pallas_call | solution.py:449

commit v7 on v6

--- a/solution.py
+++ b/solution.py
@@ -254,7 +254,6 @@
         sums[other] = pair_sum(other).astype(BF16)
         to_owner(other).start()
     pre_sum[...] = pair_sum(column) + b1[...]
-    og_onward()
 
     for copy in nb_copies:
         copy.wait()
@@ -270,6 +269,7 @@
         lane = pl.ds(pl.multiple_of(j * 128, 128), 128)
         smat_t[lane, :] = dot_last(eye[:128, :128], smat[:, lane]).astype(BF16)
 
+    og_onward()
     pl.loop(0, full // 128)(turn_smat)
 
     value = pre_sum[...]
@@ -282,6 +282,14 @@
     pre_own[...] = value.astype(BF16)
     pre_all[mine, :] = value.astype(BF16)
     onward, finish = gather(pre_own, pre_all, ag_s, ag_r)
+
+    early = (len(cols) + 1) // 2
+
+    def turn_agg(lane, size):
+        agg_t[pl.ds(lane, size), :] = dot_last(eye[:size, :size], agg[:, pl.ds(lane, size)]).astype(BF16)
+
+    by_columns(turn_agg, 0, early)
+    onward()
     for copy in late:
         copy.wait()
     og_finish()
@@ -292,14 +300,6 @@
 
     if blocks <= 2:
         steps(blocks, out_part)
-
-    onward()
-    early = (len(cols) + 1) // 2
-
-    def turn_agg(lane, size):
-        agg_t[pl.ds(lane, size), :] = dot_last(eye[:size, :size], agg[:, pl.ds(lane, size)]).astype(BF16)
-
-    by_columns(turn_agg, 0, early)
     finish()
 
     def hidden_part(i):

time: 48.3 us -> 48.3 us (level)
  no operation moved by 1% of the time
where the time goes in v7:
time: 48.3 us; the launch traced here: 48.1 us
  Pallas kernels  47.5 us (98%)
  between operations  0.64 us (1%)
    pallas_call x1, Pallas kernels, fused(): pl.pallas_call(functools.partial(kernel, n, parts, block, chunks), out_sh...  45.3 us
    pallas_call x1, Pallas kernels, finished(): pl.pallas_call(finish_kernel, out_shape=(jax.ShapeDtypeStruct(embed.shape...  2.18 us

profile of v7, /device:TPU:0, one launch (start us, length us, event | category | flops | bytes accessed | tf_op | source)
XLA Modules:
  0.0 48.1 jit_solution(15260902983869839830)
XLA Ops:
  0.6 45.3 %fused_step.1 = (bf16[64,256]{1,0:T(8,128)(2,1)}, bf16[1280,256]{1,0:T(8,128)(2,1)}) custom-call(bf16[1024,1280]{1,0:T(8,128)(2,1)} %face_hbm.1, s32[8,512]{1,0:T(8,128)} %bitcast.6, s32[1,512]{1,0:T(1,128)} %bitcast.8, bf16[1280,256]{1,0:T(8,128)(2,1)} %w1_hbm.1, f32[1,256]{1,0:T(1,128)} %bitcast.9, s32[1,128]{1,0:T(1,128)} %bitcast.10, s32[8,64]{1,0:T(8,128)} %bitcast.7, ...), custom_call_target="tpu_custom_call" | custom-call | flops 1342177280 | bytes 2621440 | tf_op jit(solution)/shard_map/fused_step/pallas_call | solution.py:484
  45.9 2.2 %finish.1 = (bf16[64,256]{1,0:T(8,128)(2,1)}, f32[1280,256]{1,0:T(8,128)}) custom-call(bf16[64,256]{1,0:T(8,128)(2,1)} %get-tuple-element.4.embed_in, bf16[1280,256]{1,0:T(8,128)(2,1)} %get-tuple-element.5.grad_in), custom_call_target="tpu_custom_call" | custom-call | tf_op jit(solution)/shard_map/finish/pallas_call | solution.py:449
